TPU v7x, 32 devices: a whole 2x2x4 slice. The times are simulated.
32 devices in a mesh: real: 2 (over x), gx: 8 (over z, y), gy: 2 (over core).
Axes of the slice: x: 2, y: 2, z: 4, core: 2. Of those that a mesh axis runs over, the one named last changes fastest.
Arguments:
- conductivity: float32 [3, 64, 128, 256], P(None, 'real', 'gx', 'gy'), parts along dimension 1, may hold values from 0.1 to 10
- part_ids: int32 [64, 128, 256], P('real', 'gx', 'gy'), parts along dimension 0, may hold values from 0 to 255, as said below
- support_mask: int32 [64, 128, 256], P('real', 'gx', 'gy'), parts along dimension 0, may hold values from 0 to 255, as said below
- well_cells: int32 [128], P('real'), parts along dimension 0, may hold values from 0 to 1048575
- well_rates: float32 [128], P('real'), parts along dimension 0, may hold values from 1 to 10
Outputs:
- basis: float32 [8, 64, 128, 256], P(None, 'real', 'gx', 'gy'), parts along dimension 1
- coarse: float32 [8, 16, 4, 8, 8], P('gx', 'gy', 'real'), parts along dimension 2
There are 2 independent parts, one for each index of `real`. A program takes and returns all parts, laid end to end along the dimension named above; each array names one. Nothing has to cross between parts.
Inputs may be any that keep to these rules, and one draw needn't show every extreme that they name: `part_ids`: along each of x, y and z, a cell's block index differs from its coordinate divided by 16 and rounded down by at most one. `support_mask`: bits 0 to 7 only; the bit of the color of the cell's own block is always set.
All inputs are finite; a program needn't handle non-finite values.
Results may differ from a plain program's by a relative error of at most 0.00011.
Values sent between devices are 32-bit elements; how exact they have to be, the bound alone decides.
A program may use at most 192 MiB of HBM per device.

v0:
```python
import jax
import jax.numpy as jnp
from jax import lax
from jax.experimental import pallas as pl
from jax.experimental.pallas import tpu as pltpu
from jax.sharding import PartitionSpec as P

NZ = 32
BLOCK = 16
SLOTS = 8
ITERS = 3
SX = 16
LY = 128
REACH = ITERS + 1
EXT = 32
TOP = 8
RB = SX + 2 * REACH
VMEM = pl.BlockSpec(memory_space=pltpu.VMEM)
RELAX = 2.0 / 3.0


def colour_of(ids):
    bx = lax.shift_right_logical(ids, 5)
    by = lax.shift_right_logical(ids, 1)
    return (bx & 1) * 4 + (by & 1) * 2 + (ids & 1)


def pack_window(get, rows):
    lane = lax.broadcasted_iota(jnp.int32, (rows, LY), 1)
    halves = []
    for zh in range(2):
        total = jnp.zeros((rows, LY), jnp.float32)
        for zl in range(16):
            moved = pltpu.roll(get(zh * 16 + zl), 8 * zl + 4, 1)
            total = jnp.where(lax.shift_right_logical(lane, 3) == zl, moved, total)
        halves.append(total)
    return halves


def pack_kernel(cond, part, mask, to_prev, to_next, mini, mini_prev, mini_next, fields):
    for f in range(3):
        fields[f] = cond[f]
    fields[3] = colour_of(part[...]).astype(jnp.float32)
    fields[4] = mask[...].astype(jnp.float32)
    to_prev[...] = fields[:, :, 0:REACH, :]
    to_next[...] = fields[:, :, SX - REACH : SX, :]
    for f in range(5):
        halves = pack_window(lambda z: fields[f, z], SX)
        for zh in range(2):
            mini[f, zh] = halves[zh]
            mini_prev[f, zh] = halves[zh][0:REACH]
            mini_next[f, zh] = halves[zh][SX - REACH : SX]


def transmit(near, far):
    total = near + far
    good = total > 0
    return jnp.where(good, 2.0 * near * far / jnp.where(good, total, 1.0), 0.0)


def main_kernel(
    cond, part, mask, above, below, mini_own, mini_y, mini_above, mini_below, wells, rates,
    out, acc,
    field, coef, diag, well_main, q_class, y_class, b0, b1,
    mfield, mcoef, mbasis, lhs, rhs, ints,
):
    gx = lax.axis_index("gx")
    gy = lax.axis_index("gy")
    ngx = lax.axis_size("gx")
    f32 = jnp.float32
    lane = lax.broadcasted_iota(jnp.int32, (EXT, LY), 1)
    zero_tile = jnp.zeros((EXT, LY), f32)

    def fill(z, carry):
        base = pl.multiple_of(z * EXT, EXT)
        own = pl.multiple_of(z * EXT + TOP, 8)
        for f in range(5):
            field[f, pl.ds(base, 8), :] = zero_tile[:8]
            field[f, pl.ds(base + 24, 8), :] = zero_tile[:8]
        ids = part[z]
        for f in range(3):
            field[f, pl.ds(own, SX), :] = cond[f, z]
        field[3, pl.ds(own, SX), :] = colour_of(ids).astype(f32)
        field[4, pl.ds(own, SX), :] = mask[z].astype(f32)
        for f in range(5):
            field[f, pl.ds(base + 4, 4), :] = above[f, z]
            field[f, pl.ds(base + 24, 4), :] = below[f, z]
        row = pl.multiple_of(z * SX, SX)
        bx = lax.shift_right_logical(ids, 5) - gx + 1
        by = (lax.shift_right_logical(ids, 1) & 15) - gy * 8 + 1
        q_class[pl.ds(row, SX), :] = (bx * 2 + (ids & 1)).astype(f32)
        y_class[pl.ds(row, SX), :] = by.astype(f32)
        ints[pl.ds(base, EXT), :] = field[4, pl.ds(base, EXT), :].astype(jnp.int32)
        return carry

    lax.fori_loop(0, NZ, fill, 0)

    side = lax.shift_right_logical(lane, 2) & 1
    for f in range(5):
        up = pack_window(lambda z: above[f, z], REACH)
        dn = pack_window(lambda z: below[f, z], REACH)
        for zh in range(2):
            at = zh * EXT
            mfield[f, at : at + 8, :] = zero_tile[:8]
            mfield[f, at + 24 : at + 32, :] = zero_tile[:8]
            mine4 = side[:REACH] == gy
            mfield[f, at + 4 : at + 8, :] = jnp.where(mine4, up[zh], mini_above[f, zh])
            mfield[f, at + 24 : at + 28, :] = jnp.where(mine4, dn[zh], mini_below[f, zh])
            mfield[f, at + 8 : at + 24, :] = jnp.where(
                side[:SX] == gy, mini_own[f, zh], mini_y[f, zh]
            )

    cells = wells[...]
    place_y = cells & 255
    place_x = lax.shift_right_logical(cells, 8) & (SX * ngx - 1)
    place_z = lax.shift_right_logical(cells, 8 + (SX * ngx).bit_length() - 1)
    row_x = place_x - gx * SX + TOP
    inside_x = (row_x >= 4) & (row_x < 28)
    nw = cells.shape[1]

    def spread(rows, row_of, lane_of, ok):
        at_row = lax.broadcasted_iota(jnp.int32, (rows, nw), 0)
        hot = jnp.where((at_row == row_of) & ok, 1.0, 0.0).astype(f32)
        at_lane = lax.broadcasted_iota(jnp.int32, (LY, nw), 0)
        val = jnp.where(at_lane == lane_of, rates[...], 0.0)
        return lax.dot_general(
            hot, val, (((1,), (1,)), ((), ())),
            precision=lax.Precision.HIGHEST, preferred_element_type=f32,
        )

    own_y = place_y - gy * LY
    well_main[...] = spread(
        NZ * EXT, place_z * EXT + row_x, own_y, inside_x & (own_y >= 0) & (own_y < LY)
    )
    col = place_y - (LY - 4)
    well_mini = spread(
        2 * EXT,
        lax.shift_right_logical(place_z, 4) * EXT + row_x,
        (place_z & 15) * 8 + col,
        inside_x & (col >= 0) & (col < 8),
    )

    def finish(flows, well):
        total = well + flows[0] + flows[1] + flows[2] + flows[3] + flows[4] + flows[5]
        total = jnp.where(total > 0, total, 1.0)
        scale = RELAX / total
        return total, [flow * scale for flow in flows]

    for zh in range(2):
        at = zh * EXT
        kx, ky, kz = (mfield[f, at : at + EXT, :] for f in range(3))
        other = mfield[2, (1 - zh) * EXT : (2 - zh) * EXT, :]
        xp = transmit(kx, pltpu.roll(kx, EXT - 1, 0))
        xm = pltpu.roll(xp, 1, 0)
        yp = transmit(ky, pltpu.roll(ky, LY - 1, 1))
        ym = pltpu.roll(yp, 1, 1)
        up = pltpu.roll(kz, LY - 8, 1)
        dn = pltpu.roll(kz, 8, 1)
        if zh == 0:
            up = jnp.where(lane < LY - 8, up, pltpu.roll(other, LY - 8, 1))
            zp = transmit(kz, up)
            zm = jnp.where(lane < 8, 0.0, transmit(kz, dn))
        else:
            dn = jnp.where(lane >= 8, dn, pltpu.roll(other, 8, 1))
            zp = jnp.where(lane < LY - 8, transmit(kz, up), 0.0)
            zm = transmit(kz, dn)
        unused, parts = finish((xm, xp, ym, yp, zm, zp), well_mini[at : at + EXT])
        for d in range(6):
            mcoef[d, at : at + EXT, :] = parts[d]

    def shift_of(z):
        return 123 + 2 * gy - 8 * (z & 15)

    def coefs(z, zm):
        base = pl.multiple_of(z * EXT, EXT)
        here = pl.ds(base, EXT)
        kx, ky, kz = (field[f, here, :] for f in range(3))
        half = pl.multiple_of(lax.shift_right_logical(z, 4) * EXT, EXT)
        edge = pltpu.roll(mfield[1, pl.ds(half, EXT), :], shift_of(z), 1)
        xp = transmit(kx, pltpu.roll(kx, EXT - 1, 0))
        xm = pltpu.roll(xp, 1, 0)
        yp = transmit(ky, jnp.where(lane == LY - 1, edge, pltpu.roll(ky, LY - 1, 1)))
        yp = jnp.where((lane == LY - 1) & (gy == 1), 0.0, yp)
        first = jnp.where(gy == 1, transmit(ky, edge), 0.0)
        ym = jnp.where(lane == 0, first, pltpu.roll(yp, 1, 1))
        later = pl.multiple_of(jnp.minimum(z + 1, NZ - 1) * EXT, EXT)
        zp = transmit(kz, field[2, pl.ds(later, EXT), :])
        zp = jnp.where(z == NZ - 1, 0.0, zp)
        total, parts = finish((xm, xp, ym, yp, zm, zp), well_main[here, :])
        diag[here, :] = total
        for d in range(6):
            coef[d, here, :] = parts[d]
        return zp

    lax.fori_loop(0, NZ, coefs, zero_tile)

    slot = lax.broadcasted_iota(jnp.int32, (SLOTS, LY), 0)
    slot_f = slot.astype(f32)
    bit = lax.shift_left(jnp.ones_like(slot), slot)
    lane8 = lax.broadcasted_iota(jnp.int32, (SLOTS, LY), 1)
    is_last = lane8 == LY - 1
    is_first = lane8 == 0
    zero8 = jnp.zeros((SLOTS, LY), f32)

    def wide(ref, row):
        return jnp.broadcast_to(ref[pl.ds(row, 1), :], (SLOTS, LY))

    for zh in range(2):
        for s in range(RB):
            mbasis[0, zh, s] = (wide(mfield.at[3], zh * EXT + 4 + s) == slot_f).astype(f32)
    for it in range(ITERS):
        mbasis[it + 1] = jnp.zeros((2, RB, SLOTS, LY), f32)

        def window(s, carry):
            both = (mbasis[it, 0, s], mbasis[it, 1, s])
            ups = [pltpu.roll(v, LY - 8, 1) for v in both]
            dns = [pltpu.roll(v, 8, 1) for v in both]
            ups[0] = jnp.where(lane8 < LY - 8, ups[0], ups[1])
            dns[1] = jnp.where(lane8 >= 8, dns[1], dns[0])
            for zh in range(2):
                row = zh * EXT + 4 + s
                value = both[zh]
                near = (
                    mbasis[it, zh, s - 1], mbasis[it, zh, s + 1],
                    pltpu.roll(value, 1, 1), pltpu.roll(value, LY - 1, 1),
                    dns[zh], ups[zh],
                )
                new = (1.0 - RELAX) * value
                for d in range(6):
                    new = new + wide(mcoef.at[d], row) * near[d]
                bits = wide(mfield.at[4], row).astype(jnp.int32) & bit
                mbasis[it + 1, zh, s] = jnp.where(bits != 0, new, 0.0)
            return carry

        lax.fori_loop(it + 1, RB - it - 1, window, 0)

    for ref in (b0, b1):
        ref[0] = jnp.zeros((RB, SLOTS, LY), f32)
        ref[NZ + 1] = jnp.zeros((RB, SLOTS, LY), f32)

    def start(z, carry):
        for s in range(RB):
            b0[z + 1, s] = (wide(field.at[3], z * EXT + 4 + s) == slot_f).astype(f32)
        return carry

    lax.fori_loop(0, NZ, start, 0)

    def spread_sum(src, it, z, s, before, value, after):
        row = z * EXT + 4 + s
        edge = pltpu.roll(mbasis[it, lax.shift_right_logical(z, 4), s], shift_of(z), 1)
        left = jnp.where(is_first, edge, pltpu.roll(value, 1, 1))
        right = jnp.where(is_last, edge, pltpu.roll(value, LY - 1, 1))
        near = (before, after, left, right, src[z, s], src[z + 2, s])
        terms = [wide(coef.at[d], row) * near[d] for d in range(6)]
        return (terms[0] + terms[1]) + (terms[2] + terms[3]) + (terms[4] + terms[5])

    for it in range(ITERS):
        src, dst = ((b0, b1), (b1, b0))[it % 2]

        def smooth(z, carry):
            before = src[z + 1, it]
            value = src[z + 1, it + 1]
            for s in range(it + 1, RB - it - 1):
                after = src[z + 1, s + 1]
                new = (1.0 - RELAX) * value + spread_sum(src, it, z, s, before, value, after)
                bits = wide(ints, z * EXT + 4 + s) & bit
                dst[z + 1, s] = jnp.where(bits != 0, new, 0.0)
                before, value = value, after
            return carry

        lax.fori_loop(0, NZ, smooth, 0)

    src = (b0, b1)[ITERS % 2]
    acc[...] = jnp.zeros_like(acc)

    def both_parts(value):
        high = value.astype(jnp.bfloat16).astype(f32)
        return high, value - high

    def gather(z, carry):
        before = src[z + 1, REACH - 1]
        value = src[z + 1, REACH]
        for x in range(SX):
            s = x + REACH
            after = src[z + 1, s + 1]
            total = spread_sum(src, ITERS, z, s, before, value, after)
            applied = wide(diag, z * EXT + 4 + s) * (value - 1.5 * total)
            out[pl.ds(z * SX + x, SLOTS, stride=NZ * SX), :] = value
            at = slice(x * LY, (x + 1) * LY)
            q = wide(q_class, z * SX + x)
            y = wide(y_class, z * SX + x)
            bh, bl = both_parts(value)
            ah, al = both_parts(applied)
            for c in range(6):
                hit = q == float(c)
                pair = jnp.concatenate([jnp.where(hit, bh, zero8), jnp.where(hit, bl, zero8)], 0)
                lhs[c * 16 : c * 16 + 16, at] = pair.astype(jnp.bfloat16)
            for c in range(10):
                hit = y == float(c)
                pair = jnp.concatenate([jnp.where(hit, ah, zero8), jnp.where(hit, al, zero8)], 0)
                rhs[c * 16 : c * 16 + 16, at] = pair.astype(jnp.bfloat16)
            before, value = value, after
        acc[...] += lax.dot_general(
            lhs[...], rhs[...], (((1,), (1,)), ((), ())), preferred_element_type=f32
        )
        return carry

    lax.fori_loop(0, NZ, gather, 0)


def body(conductivity, part_ids, support_mask, well_cells, well_rates):
    f32 = jnp.float32
    count = lax.axis_size("gx")
    shape = jax.ShapeDtypeStruct
    to_prev, to_next, mini, mini_prev, mini_next = pl.pallas_call(
        pack_kernel,
        out_shape=(
            shape((5, NZ, REACH, LY), f32),
            shape((5, NZ, REACH, LY), f32),
            shape((5, 2, SX, LY), f32),
            shape((5, 2, REACH, LY), f32),
            shape((5, 2, REACH, LY), f32),
        ),
        in_specs=[VMEM] * 3,
        out_specs=(VMEM,) * 5,
        scratch_shapes=[pltpu.VMEM((5, NZ, SX, LY), f32)],
        compiler_params=pltpu.CompilerParams(vmem_limit_bytes=32 * 2**20),
        name="pack",
    )(conductivity, part_ids, support_mask)
    down = [(i, i + 1) for i in range(count - 1)]
    up = [(i + 1, i) for i in range(count - 1)]
    flip = [(0, 1), (1, 0)]

    def cross(pairs):
        return [(a * 2 + c, b * 2 + 1 - c) for a, b in pairs for c in range(2)]

    above = lax.ppermute(to_next, "gx", down)
    below = lax.ppermute(to_prev, "gx", up)
    mini_y = lax.ppermute(mini, "gy", flip)
    mini_above = lax.ppermute(mini_next, ("gx", "gy"), cross(down))
    mini_below = lax.ppermute(mini_prev, ("gx", "gy"), cross(up))
    basis, acc = pl.pallas_call(
        main_kernel,
        out_shape=(shape((SLOTS * NZ * SX, LY), f32), shape((96, 160), f32)),
        in_specs=[VMEM] * 11,
        out_specs=(VMEM,) * 2,
        scratch_shapes=[
            pltpu.VMEM((5, NZ * EXT, LY), f32),
            pltpu.VMEM((6, NZ * EXT, LY), f32),
            pltpu.VMEM((NZ * EXT, LY), f32),
            pltpu.VMEM((NZ * EXT, LY), f32),
            pltpu.VMEM((NZ * SX, LY), f32),
            pltpu.VMEM((NZ * SX, LY), f32),
            pltpu.VMEM((NZ + 2, RB, SLOTS, LY), f32),
            pltpu.VMEM((NZ + 2, RB, SLOTS, LY), f32),
            pltpu.VMEM((5, 2 * EXT, LY), f32),
            pltpu.VMEM((6, 2 * EXT, LY), f32),
            pltpu.VMEM((ITERS + 1, 2, RB, SLOTS, LY), f32),
            pltpu.VMEM((96, SX * LY), jnp.bfloat16),
            pltpu.VMEM((160, SX * LY), jnp.bfloat16),
            pltpu.VMEM((NZ * EXT, LY), jnp.int32),
        ],
        compiler_params=pltpu.CompilerParams(vmem_limit_bytes=48 * 2**20),
        name="smooth",
    )(
        conductivity, part_ids, support_mask, above, below, mini, mini_y, mini_above, mini_below,
        well_cells.reshape(1, -1), well_rates.reshape(1, -1),
    )
    sums = acc.reshape(3, 2, 2, SLOTS, 10, 2, SLOTS).sum((2, 5))
    grid = jnp.transpose(sums, (0, 3, 1, 2, 4)).reshape(3, 10, 2, SLOTS * SLOTS)
    from_above = lax.ppermute(grid[:, 0], "gy", [(1, 0)])
    from_below = lax.ppermute(grid[:, 9], "gy", [(0, 1)])
    grid = grid.at[:, 8].add(from_above).at[:, 1].add(from_below)
    from_right = lax.ppermute(grid[0], "gx", up)
    from_left = lax.ppermute(grid[2], "gx", down)
    total = (grid[1] + from_right + from_left)[1:9]
    return (
        basis.reshape(SLOTS, NZ, SX, LY),
        total.reshape(1, 8, 2, SLOTS, SLOTS),
    )


def solution(mesh):
    placed = (
        P(None, "real", "gx", "gy"),
        P("real", "gx", "gy"),
        P("real", "gx", "gy"),
        P("real"),
        P("real"),
    )
    return jax.shard_map(
        body,
        mesh=mesh,
        in_specs=placed,
        out_specs=(P(None, "real", "gx", "gy"), P("gx", "gy", "real", None, None)),
        check_vma=False,
    )
```

profile of v0, /device:TPU:0, one launch (start us, length us, event | category | flops | bytes accessed | tf_op | source)
XLA Modules:
  0.0 90.9 jit_solution(4741870702997523748)
XLA Ops:
  0.6 1.1 %copy-done = f32[3,32,16,128]{3,2,1,0:T(8,128)S(1)} copy-done((f32[3,32,16,128]{3,2,1,0:T(8,128)S(1)}, f32[3,32,16,128]{3,2,1,0:T(8,128)}, u32[]{:S(2)}) %copy-start) | copy-done | bytes 786456
  1.8 0.9 %copy-done.2 = s32[32,16,128]{2,1,0:T(8,128)S(1)} copy-done((s32[32,16,128]{2,1,0:T(8,128)S(1)}, s32[32,16,128]{2,1,0:T(8,128)}, u32[]{:S(2)}) %copy-start.2) | copy-done | bytes 262168
  2.7 0.9 %copy-done.4 = s32[32,16,128]{2,1,0:T(8,128)S(1)} copy-done((s32[32,16,128]{2,1,0:T(8,128)S(1)}, s32[32,16,128]{2,1,0:T(8,128)}, u32[]{:S(2)}) %copy-start.4) | copy-done | bytes 262168
  3.7 0.5 pack.1
  4.2 4.9 %collective-permute-start = (f32[5,32,4,128]{3,2,1,0:T(4,128)S(1)}, f32[5,32,4,128]{3,2,1,0:T(4,128)S(1)}, u32[]{:S(2)}, u32[]{:S(2)}) collective-permute-start(f32[5,32,4,128]{3,2,1,0:T(4,128)S(1)} %get-tuple-element.33), channel_id=1, source_target_pairs={{0,2},{2,4},{4,6},{6,8},{8,10},{10,12},{12,14},{1,3},{3,5},{5,7},{... | collective-permute-start | bytes 983048 | tf_op jit(solution)/shard_map/ppermute | solution.py:337
  9.1 1.3 %collective-permute-start.1 = (f32[5,32,4,128]{3,2,1,0:T(4,128)S(1)}, f32[5,32,4,128]{3,2,1,0:T(4,128)S(1)}, u32[]{:S(2)}, u32[]{:S(2)}) collective-permute-start(f32[5,32,4,128]{3,2,1,0:T(4,128)S(1)} %get-tuple-element.34), channel_id=1, source_target_pairs={{2,0},{4,2},{6,4},{8,6},{10,8},{12,10},{14,12},{3,1},{5,3},{7,5},{... | collective-permute-start | bytes 983048 | tf_op jit(solution)/shard_map/ppermute | solution.py:338
  10.4 4.6 %collective-permute-start.3 = (f32[5,2,4,128]{3,2,1,0:T(4,128)S(1)}, f32[5,2,4,128]{3,2,1,0:T(4,128)S(1)}, u32[]{:S(2)}, u32[]{:S(2)}) collective-permute-start(f32[5,2,4,128]{3,2,1,0:T(4,128)S(1)} %get-tuple-element.36), channel_id=1, source_target_pairs={{0,3},{1,2},{2,5},{3,4},{4,7},{5,6},{6,9},{7,8},{8,11},{9,10},{10,... | collective-permute-start | bytes 61448 | tf_op jit(solution)/shard_map/ppermute | solution.py:340
  15.1 1.3 %collective-permute-start.4 = (f32[5,2,4,128]{3,2,1,0:T(4,128)S(1)}, f32[5,2,4,128]{3,2,1,0:T(4,128)S(1)}, u32[]{:S(2)}, u32[]{:S(2)}) collective-permute-start(f32[5,2,4,128]{3,2,1,0:T(4,128)S(1)} %get-tuple-element.37), channel_id=1, source_target_pairs={{2,1},{3,0},{4,3},{5,2},{6,5},{7,4},{8,7},{9,6},{10,9},{11,8},{12,... | collective-permute-start | bytes 61448 | tf_op jit(solution)/shard_map/ppermute | solution.py:341
  16.4 7.5 %collective-permute-done.3.mini_above = f32[5,2,4,128]{3,2,1,0:T(4,128)S(1)} collective-permute-done((f32[5,2,4,128]{3,2,1,0:T(4,128)S(1)}, f32[5,2,4,128]{3,2,1,0:T(4,128)S(1)}, u32[]{:S(2)}, u32[]{:S(2)}) %collective-permute-start.3) | collective-permute-done | bytes 20512 | tf_op jit(solution)/shard_map/ppermute | solution.py:340
  23.9 1.1 %copy-done.1 = f32[3,32,16,128]{3,2,1,0:T(8,128)S(1)} copy-done((f32[3,32,16,128]{3,2,1,0:T(8,128)S(1)}, f32[3,32,16,128]{3,2,1,0:T(8,128)}, u32[]{:S(2)}) %copy-start.1) | copy-done | bytes 786456
  25.1 0.9 %copy-done.3 = s32[32,16,128]{2,1,0:T(8,128)S(1)} copy-done((s32[32,16,128]{2,1,0:T(8,128)S(1)}, s32[32,16,128]{2,1,0:T(8,128)}, u32[]{:S(2)}) %copy-start.3) | copy-done | bytes 262168
  26.0 0.9 %copy-done.5 = s32[32,16,128]{2,1,0:T(8,128)S(1)} copy-done((s32[32,16,128]{2,1,0:T(8,128)S(1)}, s32[32,16,128]{2,1,0:T(8,128)}, u32[]{:S(2)}) %copy-start.5) | copy-done | bytes 262168
  27.0 0.7 copy-done.6
  27.6 0.7 copy-done.7
  28.3 44.1 %smooth.1 = (f32[4096,128]{1,0:T(8,128)}, f32[96,160]{1,0:T(8,128)S(1)}) custom-call(f32[3,32,16,128]{3,2,1,0:T(8,128)S(1)} %copy-done.1, s32[32,16,128]{2,1,0:T(8,128)S(1)} %copy-done.3, s32[32,16,128]{2,1,0:T(8,128)S(1)} %copy-done.5, f32[5,32,4,128]{3,2,1,0:T(4,128)S(1)} %collective-permute-done.above, ...), custom_call_target="tpu_custom_call" | custom-call | tf_op jit(solution)/shard_map/smooth/pallas_call | solution.py:342
  72.5 0.8 reshape.96
  73.3 1.1 %reduce_sum.9 = f32[3,2,8,10,8]{2,1,0,4,3:T(2,128)S(1)} reduce(f32[3,2,2,8,10,2,8]{3,2,1,0,6,5,4:T(2,128)S(1)} %reshape.96, f32[]{:T(128)} %constant.55.clone.1), dimensions={2,5}, to_apply=%region_0.0 | reduce | flops 11520 | bytes 76804 | tf_op jit(solution)/shard_map/reduce_sum | solution.py:369
  74.7 1.3 %collective-permute-start.5 = (f32[3,2,64]{2,1,0:T(2,128)S(1)}, f32[3,2,64]{2,1,0:T(2,128)S(1)}, u32[]{:S(2)}, u32[]{:S(2)}) collective-permute-start(f32[3,2,64]{2,1,0:T(2,128)S(1)} %slice_bitcast_fusion.4), channel_id=1, source_target_pairs={{1,0},{3,2},{5,4},{7,6},{9,8},{11,10},{13,12},{15,14},{17,16},{19,... | collective-permute-start | bytes 4616 | tf_op jit(solution)/shard_map/ppermute | solution.py:371
  76.0 3.0 %collective-permute-start.6 = (f32[3,2,64]{2,1,0:T(2,128)S(1)}, f32[3,2,64]{2,1,0:T(2,128)S(1)}, u32[]{:S(2)}, u32[]{:S(2)}) collective-permute-start(f32[3,2,64]{2,1,0:T(2,128)S(1)} %slice_bitcast_fusion.3), channel_id=1, source_target_pairs={{0,1},{2,3},{4,5},{6,7},{8,9},{10,11},{12,13},{14,15},{16,17},{18,... | collective-permute-start | bytes 4616 | tf_op jit(solution)/shard_map/ppermute | solution.py:372
  79.1 0.8 collective-permute-done.6
  79.9 4.1 %collective-permute-start.8 = (f32[10,2,64]{2,1,0:T(2,128)S(1)}, f32[10,2,64]{2,1,0:T(2,128)S(1)}, u32[]{:S(2)}, u32[]{:S(2)}) collective-permute-start(f32[10,2,64]{2,1,0:T(2,128)S(1)} %get-tuple-element.41), channel_id=1, source_target_pairs={{0,2},{2,4},{4,6},{6,8},{8,10},{10,12},{12,14},{1,3},{3,5},{5,7},{... | collective-permute-start | bytes 15368 | tf_op jit(solution)/shard_map/ppermute | solution.py:375
  84.0 1.3 %collective-permute-start.7 = (f32[10,2,64]{2,1,0:T(2,128)S(1)}, f32[10,2,64]{2,1,0:T(2,128)S(1)}, u32[]{:S(2)}, u32[]{:S(2)}) collective-permute-start(f32[10,2,64]{2,1,0:T(2,128)S(1)} %get-tuple-element.42), channel_id=1, source_target_pairs={{2,0},{4,2},{6,4},{8,6},{10,8},{12,10},{14,12},{3,1},{5,3},{7,5},{... | collective-permute-start | bytes 15368 | tf_op jit(solution)/shard_map/ppermute | solution.py:374
  85.4 4.7 %collective-permute-done.7 = f32[10,2,64]{2,1,0:T(2,128)S(1)} collective-permute-done((f32[10,2,64]{2,1,0:T(2,128)S(1)}, f32[10,2,64]{2,1,0:T(2,128)S(1)}, u32[]{:S(2)}, u32[]{:S(2)}) %collective-permute-start.7) | collective-permute-done | bytes 5152 | tf_op jit(solution)/shard_map/ppermute | solution.py:374
  90.2 0.7 reshape.100
  (25 shorter events, 0.6 us)
Async XLA Ops:
  0.6 1.1 %copy-start = (f32[3,32,16,128]{3,2,1,0:T(8,128)S(1)}, f32[3,32,16,128]{3,2,1,0:T(8,128)}, u32[]{:S(2)}) copy-start(f32[3,32,16,128]{3,2,1,0:T(8,128)} %cond.3) | copy-start | bytes 2359300
  1.8 0.9 %copy-start.2 = (s32[32,16,128]{2,1,0:T(8,128)S(1)}, s32[32,16,128]{2,1,0:T(8,128)}, u32[]{:S(2)}) copy-start(s32[32,16,128]{2,1,0:T(8,128)} %part.3) | copy-start | bytes 786436
  2.7 0.9 %copy-start.4 = (s32[32,16,128]{2,1,0:T(8,128)S(1)}, s32[32,16,128]{2,1,0:T(8,128)}, u32[]{:S(2)}) copy-start(s32[32,16,128]{2,1,0:T(8,128)} %mask.3) | copy-start | bytes 786436
  4.2 19.7 %collective-permute-start = (f32[5,32,4,128]{3,2,1,0:T(4,128)S(1)}, f32[5,32,4,128]{3,2,1,0:T(4,128)S(1)}, u32[]{:S(2)}, u32[]{:S(2)}) collective-permute-start(f32[5,32,4,128]{3,2,1,0:T(4,128)S(1)} %get-tuple-element.33), channel_id=1, source_target_pairs={{0,2},{2,4},{4,6},{6,8},{8,10},{10,12},{12,14},{1,3},{3,5},{5,7},{... | collective-permute-start | bytes 983048 | tf_op jit(solution)/shard_map/ppermute | solution.py:337
  9.1 14.8 %collective-permute-start.1 = (f32[5,32,4,128]{3,2,1,0:T(4,128)S(1)}, f32[5,32,4,128]{3,2,1,0:T(4,128)S(1)}, u32[]{:S(2)}, u32[]{:S(2)}) collective-permute-start(f32[5,32,4,128]{3,2,1,0:T(4,128)S(1)} %get-tuple-element.34), channel_id=1, source_target_pairs={{2,0},{4,2},{6,4},{8,6},{10,8},{12,10},{14,12},{3,1},{5,3},{7,5},{... | collective-permute-start | bytes 983048 | tf_op jit(solution)/shard_map/ppermute | solution.py:338
  10.4 13.5 %collective-permute-start.2 = (f32[5,2,16,128]{3,2,1,0:T(8,128)S(1)}, f32[5,2,16,128]{3,2,1,0:T(8,128)S(1)}, u32[]{:S(2)}, u32[]{:S(2)}) collective-permute-start(f32[5,2,16,128]{3,2,1,0:T(8,128)S(1)} %get-tuple-element.35.mini_own), channel_id=1, source_target_pairs={{0,1},{1,0},{2,3},{3,2},{4,5},{5,4},{6,7},{7,6},{8,9},{9,8},{10,11... | collective-permute-start | bytes 245768 | tf_op jit(solution)/shard_map/ppermute | solution.py:339
  10.4 13.5 %collective-permute-start.3 = (f32[5,2,4,128]{3,2,1,0:T(4,128)S(1)}, f32[5,2,4,128]{3,2,1,0:T(4,128)S(1)}, u32[]{:S(2)}, u32[]{:S(2)}) collective-permute-start(f32[5,2,4,128]{3,2,1,0:T(4,128)S(1)} %get-tuple-element.36), channel_id=1, source_target_pairs={{0,3},{1,2},{2,5},{3,4},{4,7},{5,6},{6,9},{7,8},{8,11},{9,10},{10,... | collective-permute-start | bytes 61448 | tf_op jit(solution)/shard_map/ppermute | solution.py:340
  15.1 8.8 %collective-permute-start.4 = (f32[5,2,4,128]{3,2,1,0:T(4,128)S(1)}, f32[5,2,4,128]{3,2,1,0:T(4,128)S(1)}, u32[]{:S(2)}, u32[]{:S(2)}) collective-permute-start(f32[5,2,4,128]{3,2,1,0:T(4,128)S(1)} %get-tuple-element.37), channel_id=1, source_target_pairs={{2,1},{3,0},{4,3},{5,2},{6,5},{7,4},{8,7},{9,6},{10,9},{11,8},{12,... | collective-permute-start | bytes 61448 | tf_op jit(solution)/shard_map/ppermute | solution.py:341
  23.9 1.1 %copy-start.1 = (f32[3,32,16,128]{3,2,1,0:T(8,128)S(1)}, f32[3,32,16,128]{3,2,1,0:T(8,128)}, u32[]{:S(2)}) copy-start(f32[3,32,16,128]{3,2,1,0:T(8,128)} %cond.3) | copy-start | bytes 2359300
  25.1 0.9 %copy-start.3 = (s32[32,16,128]{2,1,0:T(8,128)S(1)}, s32[32,16,128]{2,1,0:T(8,128)}, u32[]{:S(2)}) copy-start(s32[32,16,128]{2,1,0:T(8,128)} %part.3) | copy-start | bytes 786436
  26.0 0.9 %copy-start.5 = (s32[32,16,128]{2,1,0:T(8,128)S(1)}, s32[32,16,128]{2,1,0:T(8,128)}, u32[]{:S(2)}) copy-start(s32[32,16,128]{2,1,0:T(8,128)} %mask.3) | copy-start | bytes 786436
  27.0 0.7 copy-start.6
  27.6 0.7 copy-start.7
  74.7 4.4 %collective-permute-start.5 = (f32[3,2,64]{2,1,0:T(2,128)S(1)}, f32[3,2,64]{2,1,0:T(2,128)S(1)}, u32[]{:S(2)}, u32[]{:S(2)}) collective-permute-start(f32[3,2,64]{2,1,0:T(2,128)S(1)} %slice_bitcast_fusion.4), channel_id=1, source_target_pairs={{1,0},{3,2},{5,4},{7,6},{9,8},{11,10},{13,12},{15,14},{17,16},{19,... | collective-permute-start | bytes 4616 | tf_op jit(solution)/shard_map/ppermute | solution.py:371
  76.0 3.8 %collective-permute-start.6 = (f32[3,2,64]{2,1,0:T(2,128)S(1)}, f32[3,2,64]{2,1,0:T(2,128)S(1)}, u32[]{:S(2)}, u32[]{:S(2)}) collective-permute-start(f32[3,2,64]{2,1,0:T(2,128)S(1)} %slice_bitcast_fusion.3), channel_id=1, source_target_pairs={{0,1},{2,3},{4,5},{6,7},{8,9},{10,11},{12,13},{14,15},{16,17},{18,... | collective-permute-start | bytes 4616 | tf_op jit(solution)/shard_map/ppermute | solution.py:372
  79.9 5.5 %collective-permute-start.8 = (f32[10,2,64]{2,1,0:T(2,128)S(1)}, f32[10,2,64]{2,1,0:T(2,128)S(1)}, u32[]{:S(2)}, u32[]{:S(2)}) collective-permute-start(f32[10,2,64]{2,1,0:T(2,128)S(1)} %get-tuple-element.41), channel_id=1, source_target_pairs={{0,2},{2,4},{4,6},{6,8},{8,10},{10,12},{12,14},{1,3},{3,5},{5,7},{... | collective-permute-start | bytes 15368 | tf_op jit(solution)/shard_map/ppermute | solution.py:375
  84.0 6.1 %collective-permute-start.7 = (f32[10,2,64]{2,1,0:T(2,128)S(1)}, f32[10,2,64]{2,1,0:T(2,128)S(1)}, u32[]{:S(2)}, u32[]{:S(2)}) collective-permute-start(f32[10,2,64]{2,1,0:T(2,128)S(1)} %get-tuple-element.42), channel_id=1, source_target_pairs={{2,0},{4,2},{6,4},{8,6},{10,8},{12,10},{14,12},{3,1},{5,3},{7,5},{... | collective-permute-start | bytes 15368 | tf_op jit(solution)/shard_map/ppermute | solution.py:374
where the time goes:
time: 91.4 us; the launch traced here: 90.9 us
  Pallas kernels  44.6 us (49%)
  starting transfers between devices  21.9 us (24%)
  waiting for transfers between devices  13.1 us (14%)
  local copies, waits for them, and re-layouts  9.29 us (10%)
  other arithmetic  1.12 us (1%)
    pallas_call x1, Pallas kernels, body(): pl.pallas_call(main_kernel, out_shape=(shape((SLOTS * NZ * SX, LY), f32),...  44.1 us
    ppermute x1, waiting for transfers between devices, body(): mini_above = lax.ppermute(mini_next, ('gx', 'gy'), cross(down))  7.51 us
    unnamed x16, local copies, waits for them, and re-layouts  7.36 us
    ppermute x1, starting transfers between devices, body(): above = lax.ppermute(to_next, 'gx', down)  4.89 us
    ppermute x1, waiting for transfers between devices, body(): from_right = lax.ppermute(grid[0], 'gx', up)  4.74 us
    ppermute x1, starting transfers between devices, body(): mini_above = lax.ppermute(mini_next, ('gx', 'gy'), cross(down))  4.64 us
    ppermute x1, starting transfers between devices, body(): from_left = lax.ppermute(grid[2], 'gx', down)  4.15 us
    ppermute x1, starting transfers between devices, body(): from_below = lax.ppermute(grid[:, 9], 'gy', [(0, 1)])  3.03 us
  transfers between devices with their start and end apart: 9, of which 4 were waited for; matrix products, arithmetic and copies ran while one was open for 0% of the time, Pallas kernels for 0%

commit v1 on v0

--- a/solution.py
+++ b/solution.py
@@ -37,19 +37,141 @@
     return halves
 
 
-def pack_kernel(cond, part, mask, to_prev, to_next, mini, mini_prev, mini_next, fields):
-    for f in range(3):
-        fields[f] = cond[f]
-    fields[3] = colour_of(part[...]).astype(jnp.float32)
-    fields[4] = mask[...].astype(jnp.float32)
-    to_prev[...] = fields[:, :, 0:REACH, :]
-    to_next[...] = fields[:, :, SX - REACH : SX, :]
+FROM_PREV = [
+    (f, SX - REACH + i, TOP - REACH + i)
+    for i in range(REACH)
+    for f in ((0, 3) if i == 0 else range(5))
+]
+FROM_NEXT = [
+    (f, i, TOP + SX + i) for i in range(REACH) for f in ((0, 3) if i == REACH - 1 else range(5))
+]
+PLANES = len(FROM_PREV)
+
+
+def others(gx, gy, ngx):
+    return (
+        (gx < ngx - 1, {"gx": gx + 1, "gy": gy}),
+        (gx > 0, {"gx": gx - 1, "gy": gy}),
+        (None, {"gx": gx, "gy": 1 - gy}),
+        (gx < ngx - 1, {"gx": gx + 1, "gy": 1 - gy}),
+        (gx > 0, {"gx": gx - 1, "gy": 1 - gy}),
+    )
+
+
+def guarded(condition, action):
+    if condition is None:
+        action()
+    else:
+        pl.when(condition)(action)
+
+
+def greet(targets):
+    barrier = pltpu.get_barrier_semaphore()
+    for condition, device in targets:
+        guarded(condition, lambda: pl.semaphore_signal(
+            barrier, inc=1, device_id=device, device_id_type=pl.DeviceIdType.MESH))
+    ahead = jnp.minimum(lax.axis_size("gx") - 1 - lax.axis_index("gx"), 1)
+    pl.semaphore_wait(barrier, 1 + 2 * ahead + 2 * jnp.minimum(lax.axis_index("gx"), 1))
+
+
+def exchange_kernel(
+    cond, part, mask, mini, above, below, mini_y, mini_above, mini_below,
+    fields, part_in, mask_in, to_prev, to_next, mini_prev, mini_next, load_sem, send_sem, recv_sem,
+):
+    gx = lax.axis_index("gx")
+    gy = lax.axis_index("gy")
+    targets = others(gx, gy, lax.axis_size("gx"))
+    loads = [
+        pltpu.make_async_copy(cond, fields.at[0:3], load_sem.at[0]),
+        pltpu.make_async_copy(part, part_in, load_sem.at[1]),
+        pltpu.make_async_copy(mask, mask_in, load_sem.at[2]),
+    ]
+    for load in loads:
+        load.start()
+    has_source = (gx > 0, gx < lax.axis_size("gx") - 1)
+    for ref, source in ((above, 0), (below, 1), (mini_above, 0), (mini_below, 1)):
+        @pl.when(jnp.logical_not(has_source[source]))
+        def _():
+            ref[...] = jnp.zeros_like(ref)
+
+    for load in loads:
+        load.wait()
+    fields[3] = colour_of(part_in[...]).astype(jnp.float32)
+    fields[4] = mask_in[...].astype(jnp.float32)
+    for n, (f, row, unused) in enumerate(FROM_NEXT):
+        to_prev[n] = fields[f, pl.ds(row, NZ, stride=SX), :]
+    for n, (f, row, unused) in enumerate(FROM_PREV):
+        to_next[n] = fields[f, pl.ds(row, NZ, stride=SX), :]
+    pairs = (
+        (to_next, above), (to_prev, below), (mini, mini_y),
+        (mini_next, mini_above), (mini_prev, mini_below),
+    )
+    copies = [
+        pltpu.make_async_remote_copy(
+            src_ref=src, dst_ref=dst, send_sem=send_sem.at[n], recv_sem=recv_sem.at[n],
+            device_id=targets[n][1], device_id_type=pl.DeviceIdType.MESH,
+        )
+        for n, (src, dst) in enumerate(pairs)
+    ]
+    greet(targets)
+    for n in (0, 1):
+        guarded(targets[n][0], copies[n].start)
     for f in range(5):
-        halves = pack_window(lambda z: fields[f, z], SX)
+        halves = pack_window(lambda z: fields[f, z * SX : z * SX + SX], SX)
         for zh in range(2):
             mini[f, zh] = halves[zh]
             mini_prev[f, zh] = halves[zh][0:REACH]
             mini_next[f, zh] = halves[zh][SX - REACH : SX]
+    for n in (2, 3, 4):
+        guarded(targets[n][0], copies[n].start)
+    sources = (has_source[0], has_source[1], None, has_source[0], has_source[1])
+    for n in range(5):
+        guarded(targets[n][0], copies[n].wait_send)
+        guarded(sources[n], copies[n].wait_recv)
+
+
+def total_kernel(acc, out, grid, edge, from_prev, from_next, edge_y, edge_prev, edge_next,
+                 send_sem, recv_sem):
+    gx = lax.axis_index("gx")
+    gy = lax.axis_index("gy")
+    ngx = lax.axis_size("gx")
+    targets = others(gx, gy, ngx)
+    has_source = (gx > 0, gx < ngx - 1)
+    for ref, source in ((from_prev, 0), (from_next, 1), (edge_prev, 0), (edge_next, 1)):
+        @pl.when(jnp.logical_not(has_source[source]))
+        def _():
+            ref[...] = jnp.zeros_like(ref)
+
+    for y in range(10):
+        both = acc[y * 16 : y * 16 + 8] + acc[y * 16 + 8 : y * 16 + 16]
+        grid[y * 8 : y * 8 + 8] = both + pltpu.roll(both, LY - 8, 1)
+    edge[...] = jnp.where(gy == 1, grid[0:8], grid[72:80])
+    pairs = ((grid, from_prev), (grid, from_next), (edge, edge_y), (edge, edge_prev), (edge, edge_next))
+    copies = [
+        pltpu.make_async_remote_copy(
+            src_ref=src, dst_ref=dst, send_sem=send_sem.at[n], recv_sem=recv_sem.at[n],
+            device_id=targets[n][1], device_id_type=pl.DeviceIdType.MESH,
+        )
+        for n, (src, dst) in enumerate(pairs)
+    ]
+    greet(targets)
+    sources = (has_source[0], has_source[1], None, has_source[0], has_source[1])
+    for n in range(5):
+        guarded(targets[n][0], copies[n].start)
+    for n in range(5):
+        guarded(targets[n][0], copies[n].wait_send)
+        guarded(sources[n], copies[n].wait_recv)
+    for y in range(8):
+        at = slice(y * 8 + 8, y * 8 + 16)
+        mid, prev, after = grid[at], from_prev[at], from_next[at]
+        if y in (0, 7):
+            use = gy == (0 if y == 7 else 1)
+            mid = mid + jnp.where(use, edge_y[...], 0.0)
+            prev = prev + jnp.where(use, edge_prev[...], 0.0)
+            after = after + jnp.where(use, edge_next[...], 0.0)
+        out[y * 8 : y * 8 + 8] = (
+            pltpu.roll(mid, LY - 32, 1) + after + pltpu.roll(prev, LY - 64, 1)
+        )
 
 
 def transmit(near, far):
@@ -59,11 +181,19 @@
 
 
 def main_kernel(
-    cond, part, mask, above, below, mini_own, mini_y, mini_above, mini_below, wells, rates,
+    cond_hbm, part_hbm, mask_hbm, above, below, mini_own, mini_y, mini_above, mini_below, wells, rates,
     out, acc,
     field, coef, diag, well_main, q_class, y_class, b0, b1,
-    mfield, mcoef, mbasis, lhs, rhs, ints,
+    mfield, mcoef, mbasis, lhs, rhs, ints, cond, part, mask, load_sem,
 ):
+    loads = [
+        pltpu.make_async_copy(src, dst, load_sem.at[n])
+        for n, (src, dst) in enumerate(((cond_hbm, cond), (part_hbm, part), (mask_hbm, mask)))
+    ]
+    for load in loads:
+        load.start()
+    for load in loads:
+        load.wait()
     gx = lax.axis_index("gx")
     gy = lax.axis_index("gy")
     ngx = lax.axis_size("gx")
@@ -77,28 +207,32 @@
         for f in range(5):
             field[f, pl.ds(base, 8), :] = zero_tile[:8]
             field[f, pl.ds(base + 24, 8), :] = zero_tile[:8]
-        ids = part[z]
+        row = pl.multiple_of(z * SX, SX)
+        ids = part[pl.ds(row, SX), :]
         for f in range(3):
-            field[f, pl.ds(own, SX), :] = cond[f, z]
+            field[f, pl.ds(own, SX), :] = cond[f, pl.ds(row, SX), :]
         field[3, pl.ds(own, SX), :] = colour_of(ids).astype(f32)
-        field[4, pl.ds(own, SX), :] = mask[z].astype(f32)
-        for f in range(5):
-            field[f, pl.ds(base + 4, 4), :] = above[f, z]
-            field[f, pl.ds(base + 24, 4), :] = below[f, z]
-        row = pl.multiple_of(z * SX, SX)
+        field[4, pl.ds(own, SX), :] = mask[pl.ds(row, SX), :].astype(f32)
         bx = lax.shift_right_logical(ids, 5) - gx + 1
         by = (lax.shift_right_logical(ids, 1) & 15) - gy * 8 + 1
         q_class[pl.ds(row, SX), :] = (bx * 2 + (ids & 1)).astype(f32)
         y_class[pl.ds(row, SX), :] = by.astype(f32)
-        ints[pl.ds(base, EXT), :] = field[4, pl.ds(base, EXT), :].astype(jnp.int32)
+        ints[pl.ds(base, 8), :] = jnp.zeros((8, LY), jnp.int32)
+        ints[pl.ds(base + 24, 8), :] = jnp.zeros((8, LY), jnp.int32)
+        ints[pl.ds(own, SX), :] = mask[pl.ds(row, SX), :]
         return carry
 
     lax.fori_loop(0, NZ, fill, 0)
+    for planes, ref in ((FROM_PREV, above), (FROM_NEXT, below)):
+        for n, (f, unused, row) in enumerate(planes):
+            field[f, pl.ds(row, NZ, stride=EXT), :] = ref[n]
+            if f == 4:
+                ints[pl.ds(row, NZ, stride=EXT), :] = ref[n].astype(jnp.int32)
 
     side = lax.shift_right_logical(lane, 2) & 1
     for f in range(5):
-        up = pack_window(lambda z: above[f, z], REACH)
-        dn = pack_window(lambda z: below[f, z], REACH)
+        up = pack_window(lambda z: field[f, z * EXT + 4 : z * EXT + 8], REACH)
+        dn = pack_window(lambda z: field[f, z * EXT + 24 : z * EXT + 28], REACH)
         for zh in range(2):
             at = zh * EXT
             mfield[f, at : at + 8, :] = zero_tile[:8]
@@ -203,7 +337,7 @@
     zero8 = jnp.zeros((SLOTS, LY), f32)
 
     def wide(ref, row):
-        return jnp.broadcast_to(ref[pl.ds(row, 1), :], (SLOTS, LY))
+        return ref[pl.ds(row, SLOTS, stride=0), :]
 
     for zh in range(2):
         for s in range(RB):
@@ -232,7 +366,8 @@
                 mbasis[it + 1, zh, s] = jnp.where(bits != 0, new, 0.0)
             return carry
 
-        lax.fori_loop(it + 1, RB - it - 1, window, 0)
+        for s in range(it + 1, RB - it - 1):
+            window(s, 0)
 
     for ref in (b0, b1):
         ref[0] = jnp.zeros((RB, SLOTS, LY), f32)
@@ -272,6 +407,13 @@
 
     src = (b0, b1)[ITERS % 2]
     acc[...] = jnp.zeros_like(acc)
+    lhs[96:LY] = jnp.zeros((LY - 96, SX * LY), jnp.bfloat16)
+
+    zero16 = jnp.zeros((2 * SLOTS, LY), jnp.bfloat16)
+
+    def wide16(ref, row):
+        one = wide(ref, row)
+        return jnp.concatenate([one, one], 0).astype(jnp.bfloat16)
 
     def both_parts(value):
         high = value.astype(jnp.bfloat16).astype(f32)
@@ -287,21 +429,17 @@
             applied = wide(diag, z * EXT + 4 + s) * (value - 1.5 * total)
             out[pl.ds(z * SX + x, SLOTS, stride=NZ * SX), :] = value
             at = slice(x * LY, (x + 1) * LY)
-            q = wide(q_class, z * SX + x)
-            y = wide(y_class, z * SX + x)
-            bh, bl = both_parts(value)
-            ah, al = both_parts(applied)
+            q = wide16(q_class, z * SX + x)
+            y = wide16(y_class, z * SX + x)
+            b16 = jnp.concatenate(both_parts(value), 0).astype(jnp.bfloat16)
+            a16 = jnp.concatenate(both_parts(applied), 0).astype(jnp.bfloat16)
             for c in range(6):
-                hit = q == float(c)
-                pair = jnp.concatenate([jnp.where(hit, bh, zero8), jnp.where(hit, bl, zero8)], 0)
-                lhs[c * 16 : c * 16 + 16, at] = pair.astype(jnp.bfloat16)
+                lhs[c * 16 : c * 16 + 16, at] = jnp.where(q == jnp.bfloat16(c), b16, zero16)
             for c in range(10):
-                hit = y == float(c)
-                pair = jnp.concatenate([jnp.where(hit, ah, zero8), jnp.where(hit, al, zero8)], 0)
-                rhs[c * 16 : c * 16 + 16, at] = pair.astype(jnp.bfloat16)
+                rhs[c * 16 : c * 16 + 16, at] = jnp.where(y == jnp.bfloat16(c), a16, zero16)
             before, value = value, after
         acc[...] += lax.dot_general(
-            lhs[...], rhs[...], (((1,), (1,)), ((), ())), preferred_element_type=f32
+            rhs[...], lhs[...], (((1,), (1,)), ((), ())), preferred_element_type=f32
         )
         return carry
 
@@ -310,39 +448,43 @@
 
 def body(conductivity, part_ids, support_mask, well_cells, well_rates):
     f32 = jnp.float32
-    count = lax.axis_size("gx")
+    conductivity = conductivity.reshape(3, NZ * SX, LY)
+    part_ids = part_ids.reshape(NZ * SX, LY)
+    support_mask = support_mask.reshape(NZ * SX, LY)
     shape = jax.ShapeDtypeStruct
-    to_prev, to_next, mini, mini_prev, mini_next = pl.pallas_call(
-        pack_kernel,
+    mini, above, below, mini_y, mini_above, mini_below = pl.pallas_call(
+        exchange_kernel,
         out_shape=(
-            shape((5, NZ, REACH, LY), f32),
-            shape((5, NZ, REACH, LY), f32),
+            shape((5, 2, SX, LY), f32),
+            shape((PLANES, NZ, LY), f32),
+            shape((PLANES, NZ, LY), f32),
             shape((5, 2, SX, LY), f32),
             shape((5, 2, REACH, LY), f32),
             shape((5, 2, REACH, LY), f32),
         ),
-        in_specs=[VMEM] * 3,
-        out_specs=(VMEM,) * 5,
-        scratch_shapes=[pltpu.VMEM((5, NZ, SX, LY), f32)],
-        compiler_params=pltpu.CompilerParams(vmem_limit_bytes=32 * 2**20),
-        name="pack",
+        in_specs=[pl.BlockSpec(memory_space=pl.ANY)] * 3,
+        out_specs=(VMEM,) * 6,
+        scratch_shapes=[
+            pltpu.VMEM((5, NZ * SX, LY), f32),
+            pltpu.VMEM((NZ * SX, LY), jnp.int32),
+            pltpu.VMEM((NZ * SX, LY), jnp.int32),
+            pltpu.VMEM((PLANES, NZ, LY), f32),
+            pltpu.VMEM((PLANES, NZ, LY), f32),
+            pltpu.VMEM((5, 2, REACH, LY), f32),
+            pltpu.VMEM((5, 2, REACH, LY), f32),
+            pltpu.SemaphoreType.DMA((3,)),
+            pltpu.SemaphoreType.DMA((5,)),
+            pltpu.SemaphoreType.DMA((5,)),
+        ],
+        compiler_params=pltpu.CompilerParams(
+            vmem_limit_bytes=60 * 2**20, collective_id=0, has_side_effects=True
+        ),
+        name="exchange",
     )(conductivity, part_ids, support_mask)
-    down = [(i, i + 1) for i in range(count - 1)]
-    up = [(i + 1, i) for i in range(count - 1)]
-    flip = [(0, 1), (1, 0)]
-
-    def cross(pairs):
-        return [(a * 2 + c, b * 2 + 1 - c) for a, b in pairs for c in range(2)]
-
-    above = lax.ppermute(to_next, "gx", down)
-    below = lax.ppermute(to_prev, "gx", up)
-    mini_y = lax.ppermute(mini, "gy", flip)
-    mini_above = lax.ppermute(mini_next, ("gx", "gy"), cross(down))
-    mini_below = lax.ppermute(mini_prev, ("gx", "gy"), cross(up))
     basis, acc = pl.pallas_call(
         main_kernel,
-        out_shape=(shape((SLOTS * NZ * SX, LY), f32), shape((96, 160), f32)),
-        in_specs=[VMEM] * 11,
+        out_shape=(shape((SLOTS * NZ * SX, LY), f32), shape((160, LY), f32)),
+        in_specs=[pl.BlockSpec(memory_space=pl.ANY)] * 3 + [VMEM] * 8,
         out_specs=(VMEM,) * 2,
         scratch_shapes=[
             pltpu.VMEM((5, NZ * EXT, LY), f32),
@@ -356,24 +498,41 @@
             pltpu.VMEM((5, 2 * EXT, LY), f32),
             pltpu.VMEM((6, 2 * EXT, LY), f32),
             pltpu.VMEM((ITERS + 1, 2, RB, SLOTS, LY), f32),
-            pltpu.VMEM((96, SX * LY), jnp.bfloat16),
+            pltpu.VMEM((LY, SX * LY), jnp.bfloat16),
             pltpu.VMEM((160, SX * LY), jnp.bfloat16),
             pltpu.VMEM((NZ * EXT, LY), jnp.int32),
+            pltpu.VMEM((3, NZ * SX, LY), f32),
+            pltpu.VMEM((NZ * SX, LY), jnp.int32),
+            pltpu.VMEM((NZ * SX, LY), jnp.int32),
+            pltpu.SemaphoreType.DMA((3,)),
         ],
-        compiler_params=pltpu.CompilerParams(vmem_limit_bytes=48 * 2**20),
+        compiler_params=pltpu.CompilerParams(vmem_limit_bytes=60 * 2**20),
         name="smooth",
     )(
         conductivity, part_ids, support_mask, above, below, mini, mini_y, mini_above, mini_below,
         well_cells.reshape(1, -1), well_rates.reshape(1, -1),
     )
-    sums = acc.reshape(3, 2, 2, SLOTS, 10, 2, SLOTS).sum((2, 5))
-    grid = jnp.transpose(sums, (0, 3, 1, 2, 4)).reshape(3, 10, 2, SLOTS * SLOTS)
-    from_above = lax.ppermute(grid[:, 0], "gy", [(1, 0)])
-    from_below = lax.ppermute(grid[:, 9], "gy", [(0, 1)])
-    grid = grid.at[:, 8].add(from_above).at[:, 1].add(from_below)
-    from_right = lax.ppermute(grid[0], "gx", up)
-    from_left = lax.ppermute(grid[2], "gx", down)
-    total = (grid[1] + from_right + from_left)[1:9]
+    sums = pl.pallas_call(
+        total_kernel,
+        out_shape=shape((64, LY), f32),
+        in_specs=[VMEM],
+        out_specs=VMEM,
+        scratch_shapes=[
+            pltpu.VMEM((80, LY), f32),
+            pltpu.VMEM((8, LY), f32),
+            pltpu.VMEM((80, LY), f32),
+            pltpu.VMEM((80, LY), f32),
+            pltpu.VMEM((8, LY), f32),
+            pltpu.VMEM((8, LY), f32),
+            pltpu.VMEM((8, LY), f32),
+            pltpu.SemaphoreType.DMA((5,)),
+            pltpu.SemaphoreType.DMA((5,)),
+        ],
+        compiler_params=pltpu.CompilerParams(collective_id=1, has_side_effects=True),
+        name="total",
+    )(acc)
+    sums = sums[:, :32].reshape(8, SLOTS, 2, 2, SLOTS)[:, :, :, 0]
+    total = jnp.transpose(sums, (0, 2, 3, 1))
     return (
         basis.reshape(SLOTS, NZ, SX, LY),
         total.reshape(1, 8, 2, SLOTS, SLOTS),

time: 91.4 us -> 70.7 us (0.77)
  Pallas kernels: 44.6 us -> 68.2 us
  starting transfers between devices: 21.9 us -> 0 us
  waiting for transfers between devices: 13.1 us -> 0 us
  local copies, waits for them, and re-layouts: 9.29 us -> 1.58 us
  other arithmetic: 1.12 us -> 0 us
    pallas_call x1 -> x2, Pallas kernels: 0.49 us -> 27.6 us  [the longest x1 19 us: body(): pl.pallas_call(exchange_kernel, out_shape=(shape((5, 2, SX, LY), f32), sh...]
    ppermute x9 -> x0, starting transfers between devices: 21.9 us -> none  [the longest x1 4.89 us: body(): above = lax.ppermute(to_next, 'gx', down)]
    ppermute x9 -> x0, waiting for transfers between devices: 13.1 us -> none  [the longest x1 7.51 us: body(): mini_above = lax.ppermute(mini_next, ('gx', 'gy'), cross(down))]
    unnamed x16 -> x1, local copies, waits for them, and re-layouts: 7.36 us -> 0.64 us
    pallas_call x1, Pallas kernels: 44.1 us -> 40.6 us  [body(): pl.pallas_call(main_kernel, out_shape=(shape((SLOTS * NZ * SX, LY), f32),...]
    reduce_sum x1 -> x0, other arithmetic: 1.09 us -> none  [body(): sums = acc.reshape(3, 2, 2, SLOTS, 10, 2, SLOTS).sum((2, 5))]
  transfers between devices with their start and end apart: 9 -> 0, of which waited for: 4 -> 0; matrix products, arithmetic and copies ran while one was open for 0% -> 0% of each run, Pallas kernels for 0% -> 0%
where the time goes in v1:
time: 70.7 us; the launch traced here: 70.5 us
  Pallas kernels  68.2 us (96%)
  local copies, waits for them, and re-layouts  1.58 us (2%)
    pallas_call x1, Pallas kernels, body(): pl.pallas_call(main_kernel, out_shape=(shape((SLOTS * NZ * SX, LY), f32),...  40.6 us
    pallas_call x1, Pallas kernels, body(): pl.pallas_call(exchange_kernel, out_shape=(shape((5, 2, SX, LY), f32), sh...  19 us
    pallas_call x1, Pallas kernels, body(): pl.pallas_call(total_kernel, out_shape=shape((64, LY), f32), in_specs=[VM...  8.61 us

profile of v1, /device:TPU:0, one launch (start us, length us, event | category | flops | bytes accessed | tf_op | source)
XLA Modules:
  0.0 70.5 jit_solution(12673227970899739798)
XLA Ops:
  0.6 19.0 %exchange.1 = (f32[5,2,16,128]{3,2,1,0:T(8,128)}, f32[17,32,128]{2,1,0:T(8,128)}, f32[17,32,128]{2,1,0:T(8,128)}, f32[5,2,16,128]{3,2,1,0:T(8,128)}, f32[5,2,4,128]{3,2,1,0:T(4,128)}, /*index=5*/f32[5,2,4,128]{3,2,1,0:T(4,128)}) custom-call(f32[3,512,128]{2,1,0:T(8,128)} %bitcast.15, s32[512,128]{1,0:T(8,128)} %bitcast.17, s32[512,128]{1,0:T(8,128)} %bitcast.19), custom_call_target="tpu_custom_call" | custom-call | tf_op jit(solution)/shard_map/exchange/pallas_call | solution.py:455
  19.6 40.6 %smooth.1 = (f32[4096,128]{1,0:T(8,128)}, f32[160,128]{1,0:T(8,128)}) custom-call(f32[3,512,128]{2,1,0:T(8,128)} %bitcast.16, s32[512,128]{1,0:T(8,128)} %bitcast.18, s32[512,128]{1,0:T(8,128)} %bitcast.20, f32[17,32,128]{2,1,0:T(8,128)} %get-tuple-element.10.above, f32[17,32,128]{2,1,0:T(8,128)} %get-tuple-element.11.below, ...), custom_call_target="tpu_custom_call" | custom-call | tf_op jit(solution)/shard_map/smooth/pallas_call | solution.py:484
  60.2 8.6 %total.1 = f32[64,128]{1,0:T(8,128)} custom-call(f32[160,128]{1,0:T(8,128)} %get-tuple-element.17.acc), custom_call_target="tpu_custom_call" | custom-call | tf_op jit(solution)/shard_map/total/pallas_call | solution.py:515
  68.9 0.8 %copy.8 = f32[64,32]{0,1:T(8,128)S(1)} copy(f32[64,32]{1,0:T(8,128)} %bitcast.21) | data formatting | bytes 16384 | tf_op jit(solution)/shard_map/slice | solution.py:534
  69.7 0.1 reshape.34
  69.8 0.6 copy.9
  (1 shorter events, 0.0 us)

commit v2 on v1

--- a/solution.py
+++ b/solution.py
@@ -184,7 +184,7 @@
     cond_hbm, part_hbm, mask_hbm, above, below, mini_own, mini_y, mini_above, mini_below, wells, rates,
     out, acc,
     field, coef, diag, well_main, q_class, y_class, b0, b1,
-    mfield, mcoef, mbasis, lhs, rhs, ints, cond, part, mask, load_sem,
+    mfield, mcoef, mbasis, lhs0, rhs0, lhs1, rhs1, turned, ints, cond, part, mask, load_sem,
 ):
     loads = [
         pltpu.make_async_copy(src, dst, load_sem.at[n])
@@ -222,7 +222,7 @@
         ints[pl.ds(own, SX), :] = mask[pl.ds(row, SX), :]
         return carry
 
-    lax.fori_loop(0, NZ, fill, 0)
+    lax.fori_loop(0, NZ, fill, 0, unroll=4)
     for planes, ref in ((FROM_PREV, above), (FROM_NEXT, below)):
         for n, (f, unused, row) in enumerate(planes):
             field[f, pl.ds(row, NZ, stride=EXT), :] = ref[n]
@@ -326,7 +326,7 @@
             coef[d, here, :] = parts[d]
         return zp
 
-    lax.fori_loop(0, NZ, coefs, zero_tile)
+    lax.fori_loop(0, NZ, coefs, zero_tile, unroll=4)
 
     slot = lax.broadcasted_iota(jnp.int32, (SLOTS, LY), 0)
     slot_f = slot.astype(f32)
@@ -378,7 +378,7 @@
             b0[z + 1, s] = (wide(field.at[3], z * EXT + 4 + s) == slot_f).astype(f32)
         return carry
 
-    lax.fori_loop(0, NZ, start, 0)
+    lax.fori_loop(0, NZ, start, 0, unroll=2)
 
     def spread_sum(src, it, z, s, before, value, after):
         row = z * EXT + 4 + s
@@ -403,11 +403,19 @@
                 before, value = value, after
             return carry
 
-        lax.fori_loop(0, NZ, smooth, 0)
+        lax.fori_loop(0, NZ, smooth, 0, unroll=4)
 
     src = (b0, b1)[ITERS % 2]
     acc[...] = jnp.zeros_like(acc)
-    lhs[96:LY] = jnp.zeros((LY - 96, SX * LY), jnp.bfloat16)
+    turned[...] = jnp.zeros_like(turned)
+    lhs1[...] = jnp.zeros_like(lhs1)
+    rhs1[...] = jnp.zeros_like(rhs1)
+
+    def multiply(lhs, rhs):
+        turned[...] += lax.dot_general(
+            lhs[...], rhs[...], (((1,), (1,)), ((), ())), preferred_element_type=f32
+        )
+
 
     zero16 = jnp.zeros((2 * SLOTS, LY), jnp.bfloat16)
 
@@ -419,7 +427,7 @@
         high = value.astype(jnp.bfloat16).astype(f32)
         return high, value - high
 
-    def gather(z, carry):
+    def gather(z, lhs, rhs):
         before = src[z + 1, REACH - 1]
         value = src[z + 1, REACH]
         for x in range(SX):
@@ -438,12 +446,17 @@
             for c in range(10):
                 rhs[c * 16 : c * 16 + 16, at] = jnp.where(y == jnp.bfloat16(c), a16, zero16)
             before, value = value, after
-        acc[...] += lax.dot_general(
-            rhs[...], lhs[...], (((1,), (1,)), ((), ())), preferred_element_type=f32
-        )
+
+    def gather_two(t, carry):
+        multiply(lhs1, rhs1)
+        gather(2 * t, lhs0, rhs0)
+        multiply(lhs0, rhs0)
+        gather(2 * t + 1, lhs1, rhs1)
         return carry
 
-    lax.fori_loop(0, NZ, gather, 0)
+    lax.fori_loop(0, NZ // 2, gather_two, 0)
+    multiply(lhs1, rhs1)
+    acc[:, :96] = jnp.transpose(turned[...])
 
 
 def body(conductivity, part_ids, support_mask, well_cells, well_rates):
@@ -498,8 +511,11 @@
             pltpu.VMEM((5, 2 * EXT, LY), f32),
             pltpu.VMEM((6, 2 * EXT, LY), f32),
             pltpu.VMEM((ITERS + 1, 2, RB, SLOTS, LY), f32),
-            pltpu.VMEM((LY, SX * LY), jnp.bfloat16),
+            pltpu.VMEM((96, SX * LY), jnp.bfloat16),
             pltpu.VMEM((160, SX * LY), jnp.bfloat16),
+            pltpu.VMEM((96, SX * LY), jnp.bfloat16),
+            pltpu.VMEM((160, SX * LY), jnp.bfloat16),
+            pltpu.VMEM((96, 160), f32),
             pltpu.VMEM((NZ * EXT, LY), jnp.int32),
             pltpu.VMEM((3, NZ * SX, LY), f32),
             pltpu.VMEM((NZ * SX, LY), jnp.int32),

time: 70.7 us -> 57.9 us (0.82)
  Pallas kernels: 68.2 us -> 55.4 us
    pallas_call x1, Pallas kernels: 40.6 us -> 27.8 us  [body(): pl.pallas_call(main_kernel, out_shape=(shape((SLOTS * NZ * SX, LY), f32),...]
where the time goes in v2:
time: 57.9 us; the launch traced here: 57.6 us
  Pallas kernels  55.4 us (96%)
  local copies, waits for them, and re-layouts  1.58 us (3%)
  between operations  0.67 us (1%)
    pallas_call x1, Pallas kernels, body(): pl.pallas_call(main_kernel, out_shape=(shape((SLOTS * NZ * SX, LY), f32),...  27.8 us
    pallas_call x1, Pallas kernels, body(): pl.pallas_call(exchange_kernel, out_shape=(shape((5, 2, SX, LY), f32), sh...  19 us
    pallas_call x1, Pallas kernels, body(): pl.pallas_call(total_kernel, out_shape=shape((64, LY), f32), in_specs=[VM...  8.61 us

profile of v2, /device:TPU:0, one launch (start us, length us, event | category | flops | bytes accessed | tf_op | source)
XLA Modules:
  0.0 57.6 jit_solution(16355485300865885031)
XLA Ops:
  0.6 19.0 %exchange.1 = (f32[5,2,16,128]{3,2,1,0:T(8,128)}, f32[17,32,128]{2,1,0:T(8,128)}, f32[17,32,128]{2,1,0:T(8,128)}, f32[5,2,16,128]{3,2,1,0:T(8,128)}, f32[5,2,4,128]{3,2,1,0:T(4,128)}, /*index=5*/f32[5,2,4,128]{3,2,1,0:T(4,128)}) custom-call(f32[3,512,128]{2,1,0:T(8,128)} %bitcast.15, s32[512,128]{1,0:T(8,128)} %bitcast.17, s32[512,128]{1,0:T(8,128)} %bitcast.19), custom_call_target="tpu_custom_call" | custom-call | tf_op jit(solution)/shard_map/exchange/pallas_call | solution.py:468
  19.6 27.8 %smooth.1 = (f32[4096,128]{1,0:T(8,128)}, f32[160,128]{1,0:T(8,128)}) custom-call(f32[3,512,128]{2,1,0:T(8,128)} %bitcast.16, s32[512,128]{1,0:T(8,128)} %bitcast.18, s32[512,128]{1,0:T(8,128)} %bitcast.20, f32[17,32,128]{2,1,0:T(8,128)} %get-tuple-element.10.above, f32[17,32,128]{2,1,0:T(8,128)} %get-tuple-element.11.below, ...), custom_call_target="tpu_custom_call" | custom-call | tf_op jit(solution)/shard_map/smooth/pallas_call | solution.py:497
  47.4 8.6 %total.1 = f32[64,128]{1,0:T(8,128)} custom-call(f32[160,128]{1,0:T(8,128)} %get-tuple-element.17.acc), custom_call_target="tpu_custom_call" | custom-call | tf_op jit(solution)/shard_map/total/pallas_call | solution.py:531
  56.0 0.8 %copy.8 = f32[64,32]{0,1:T(8,128)S(1)} copy(f32[64,32]{1,0:T(8,128)} %bitcast.21) | data formatting | bytes 16384 | tf_op jit(solution)/shard_map/slice | solution.py:550
  56.9 0.1 reshape.34
  57.0 0.6 %copy.9 = f32[1,8,2,8,8]{4,3,2,1,0:T(8,128)} copy(f32[1,8,2,8,8]{4,1,3,2,0:T(8,128)S(1)} %slice_bitcast_fusion) | data formatting | bytes 8192
  (1 shorter events, 0.0 us)
